TPU v7x, 32 devices: a whole 2x2x4 slice. The times are simulated.
32 devices in a mesh: groups: 2 (over x), gx: 16 (over z, y, core).
Axes of the slice: x: 2, y: 2, z: 4, core: 2. Of those that a mesh axis runs over, the one named last changes fastest.
Arguments:
- particle_state: float32 [6, 8192], P(None, ('groups', 'gx')), parts along dimension 1, may hold values from -6 to 6
- neighbours: int32 [2, 24, 8192], P(None, None, ('groups', 'gx')), parts along dimension 2, may hold values from 0 to 511
- neighbour_mask: int32 [2, 24, 8192], P(None, None, ('groups', 'gx')), parts along dimension 2, may hold values 0 or 1
- face_rows: int32 [2, 2, 4096], P(None, None, ('groups', 'gx')), parts along dimension 2, may hold values from 0 to 255
- migrants: int32 [1, 2, 1024], P(None, None, ('groups', 'gx')), parts along dimension 2, may hold values from 0 to 255
- new_order: int32 [1, 8192], P(None, ('groups', 'gx')), parts along dimension 1, may hold values from 0 to 319
- loss_weights: float32 [2, 6, 8192], P(None, None, ('groups', 'gx')), parts along dimension 2, may hold values from -6 to 6
- encoder: float32 [64, 3], replicated, may hold values from -3.5 to 3.5
- pair_weights: float32 [2, 2, 64, 64], replicated, may hold values from -0.75 to 0.75
- geometry_weights: float32 [2, 64, 4], replicated, may hold values from -3 to 3
- message_weights: float32 [2, 64, 64], replicated, may hold values from -0.75 to 0.75
- update_weights: float32 [2, 64, 128], replicated, may hold values from -0.5 to 0.5
- update_gain: float32 [2, 64], replicated, may hold values from 0.1 to 1.9
- decoder: float32 [3, 64], replicated, may hold values from -0.75 to 0.75
Outputs:
- state_grad: float32 [6, 8192], P(None, ('groups', 'gx')), parts along dimension 1
- pair_grad: float32 [4, 2, 64, 64], P('groups'), parts along dimension 0
- message_grad: float32 [4, 64, 64], P('groups'), parts along dimension 0
- update_grad: float32 [4, 64, 128], P('groups'), parts along dimension 0
There are 2 independent parts, one for each index of `groups`. A program takes and returns all parts, laid end to end along the dimension named above; an argument that names none is the same for every part. Nothing has to cross between parts.
Inputs may be any that keep to these rules, and one draw needn't show every extreme that they name: `neighbours`: index the slab's own 256 particles, then 128 from the slab below, then 128 from the slab above. `face_rows`: local particle rows. `migrants`: local particle rows. `new_order`: index the slab's 256 particles, then 32 from below, then 32 from above.
All inputs are finite; a program needn't handle non-finite values. No bound on the sum of `neighbour_mask` on one device may be relied on, other than what follows from the above.
Results may differ from a plain program's by a relative error of at most 0.0001.
Values sent between devices are 32-bit elements; how exact they have to be, the bound alone decides.
A program may use at most 128 MiB of HBM per device.

v0:
```python
from functools import partial
import math

import jax
import jax.numpy as jnp
from jax import lax
from jax.sharding import PartitionSpec as P

HIGHEST = lax.Precision.HIGHEST
TIME_STEP = 0.5
EPSILON = 1e-05


def padded(array, sides, width):
    for axis, dim in sides:
        size, length = (lax.axis_size(axis), array.shape[dim])
        up = [(i, (i + 1) % size) for i in range(size - 1)]
        down = [(j, i) for i, j in up]
        last = lax.slice_in_dim(array, length - width, length, axis=dim)
        initial = lax.slice_in_dim(array, 0, width, axis=dim)
        before = lax.ppermute(last, axis, up)
        after = lax.ppermute(initial, axis, down)
        array = jnp.concatenate([before, array, after], axis=dim)
    return array


def apply_layer(
    places,
    latent,
    halo_part,
    pair_layer,
    message_layer,
    update_layer,
    geometry_layer,
    gain_layer,
    neighbour_rows,
    mask_rows,
):
    features = latent.shape[0]
    row_total = latent.shape[1]
    slot_total = neighbour_rows.shape[0]
    joined = jnp.concatenate([jnp.concatenate([places, latent], axis=0), halo_part], axis=1)
    projected = jnp.dot(pair_layer[1], joined[3:], precision=HIGHEST)
    flat_index = neighbour_rows.reshape(-1)
    senders = jnp.take(projected, flat_index, axis=1).reshape(features, slot_total, row_total)
    sender_places = jnp.take(joined[:3], flat_index, axis=1).reshape(3, slot_total, row_total)
    offsets = sender_places - places[:, None, :]
    distance = jnp.sqrt(jnp.sum(offsets * offsets, axis=0, keepdims=True) + 1.0)
    geometry = jnp.concatenate([offsets, distance], axis=0)
    own_part = jnp.dot(pair_layer[0], latent, precision=HIGHEST)
    pre_act = (
        own_part[:, None, :]
        + senders
        + jnp.einsum("of,fkp->okp", geometry_layer, geometry, precision=HIGHEST)
    )
    edge_hidden = jax.nn.silu(pre_act)
    messages = jax.nn.silu(jnp.einsum("oh,hkp->okp", message_layer, edge_hidden, precision=HIGHEST))
    collected = jnp.sum(messages * mask_rows[None], axis=1) / slot_total
    update = jnp.dot(update_layer, jnp.concatenate([latent, collected], axis=0), precision=HIGHEST)
    centred = update - jnp.mean(update, axis=0, keepdims=True)
    normed = centred * lax.rsqrt(jnp.mean(centred * centred, axis=0, keepdims=True) + EPSILON)
    return latent + gain_layer[:, None] * normed


def send_faces(joined, upward, downward):
    rim_rows = upward.shape[0]
    outgoing = jnp.concatenate(
        [jnp.take(joined, downward, axis=1), jnp.take(joined, upward, axis=1)], axis=1
    )
    widened = padded(outgoing, (("gx", 1),), rim_rows)
    return jnp.concatenate([widened[:, :rim_rows], widened[:, 3 * rim_rows :]], axis=1)


def settle(widened, upward, downward, part_rows):
    rim_rows = upward.shape[0]
    result = jnp.zeros((widened.shape[0], part_rows), jnp.float32)
    result = result.at[:, downward].add(widened[:, :rim_rows])
    return result.at[:, upward].add(widened[:, 3 * rim_rows :])


def migrate(advanced, upward, downward, order_rows):
    rim_rows = upward.shape[0]
    outgoing = jnp.concatenate(
        [jnp.take(advanced, downward, axis=1), jnp.take(advanced, upward, axis=1)], axis=1
    )
    widened = padded(outgoing, (("gx", 1),), rim_rows)
    extended = jnp.concatenate(
        [advanced, widened[:, :rim_rows], widened[:, 3 * rim_rows :]], axis=1
    )
    return jnp.take(extended, order_rows, axis=1)


def migrate_back(cotangent, upward, downward, order_rows):
    rim_rows = upward.shape[0]
    part_rows = cotangent.shape[1]
    spread = (
        jnp.zeros((cotangent.shape[0], part_rows + 2 * rim_rows), jnp.float32)
        .at[:, order_rows]
        .add(cotangent)
    )
    widened = padded(spread[:, part_rows:], (("gx", 1),), rim_rows)
    return spread[:, :part_rows] + settle(widened, upward, downward, part_rows)


def local(
    particle_state,
    neighbours,
    neighbour_mask,
    face_rows,
    migrants,
    new_order,
    loss_weights,
    encoder,
    pair_weights,
    geometry_weights,
    message_weights,
    update_weights,
    update_gain,
    decoder,
):
    steps_total = neighbours.shape[0]
    layers_total = pair_weights.shape[0]
    part_rows = particle_state.shape[1]
    mask_all = neighbour_mask.astype(jnp.float32)
    current = particle_state
    history = []
    for step_index in range(steps_total):
        upward = face_rows[step_index, 0]
        downward = face_rows[step_index, 1]
        places = current[:3]
        speeds = current[3:]
        latent = jnp.dot(encoder, speeds, precision=HIGHEST)
        records = []
        for layer_index in range(layers_total):
            halo_part = send_faces(jnp.concatenate([places, latent], axis=0), upward, downward)
            records.append((latent, halo_part))
            latent = apply_layer(
                places,
                latent,
                halo_part,
                pair_weights[layer_index],
                message_weights[layer_index],
                update_weights[layer_index],
                geometry_weights[layer_index],
                update_gain[layer_index],
                neighbours[step_index],
                mask_all[step_index],
            )
        acceleration = jnp.dot(decoder, latent, precision=HIGHEST)
        speeds_new = speeds + TIME_STEP * acceleration
        places_new = places + TIME_STEP * speeds_new
        history.append((places, records))
        if step_index + 1 < steps_total:
            advanced = jnp.concatenate([places_new, speeds_new], axis=0)
            current = migrate(
                advanced, migrants[step_index, 0], migrants[step_index, 1], new_order[step_index]
            )
    grad_pair = jnp.zeros(pair_weights.shape, jnp.float32)
    grad_message = jnp.zeros(message_weights.shape, jnp.float32)
    grad_update = jnp.zeros(update_weights.shape, jnp.float32)
    carried = jnp.zeros(particle_state.shape, jnp.float32)
    state_grad = carried
    for step_index in reversed(range(steps_total)):
        upward = face_rows[step_index, 0]
        downward = face_rows[step_index, 1]
        places, records = history[step_index]
        grad_out = loss_weights[step_index] + carried
        grad_places = grad_out[:3]
        grad_speeds = grad_out[3:] + TIME_STEP * grad_places
        grad_latent = jnp.dot(decoder.T, TIME_STEP * grad_speeds, precision=HIGHEST)
        for layer_index in reversed(range(layers_total)):
            latent_in, stored = records[layer_index]
            halo_part = stored
            local_layer = partial(
                apply_layer,
                geometry_layer=geometry_weights[layer_index],
                gain_layer=update_gain[layer_index],
                neighbour_rows=neighbours[step_index],
                mask_rows=mask_all[step_index],
            )
            _, pullback = jax.vjp(
                local_layer,
                places,
                latent_in,
                halo_part,
                pair_weights[layer_index],
                message_weights[layer_index],
                update_weights[layer_index],
            )
            grad_here, grad_prior, grad_halo, grad_pw, grad_mw, grad_uw = pullback(grad_latent)
            rim_rows = upward.shape[0]
            returned = padded(grad_halo, (("gx", 1),), rim_rows)
            spread = settle(returned, upward, downward, part_rows)
            grad_places = grad_places + grad_here + spread[:3]
            grad_latent = grad_prior + spread[3:]
            grad_pair = grad_pair.at[layer_index].add(grad_pw)
            grad_message = grad_message.at[layer_index].add(grad_mw)
            grad_update = grad_update.at[layer_index].add(grad_uw)
        grad_speeds = grad_speeds + jnp.dot(encoder.T, grad_latent, precision=HIGHEST)
        grad_current = jnp.concatenate([grad_places, grad_speeds], axis=0)
        if step_index > 0:
            carried = migrate_back(
                grad_current,
                migrants[step_index - 1, 0],
                migrants[step_index - 1, 1],
                new_order[step_index - 1],
            )
        else:
            state_grad = grad_current
    grad_pair, grad_message, grad_update = lax.psum((grad_pair, grad_message, grad_update), "gx")
    factor = 1.0 / math.sqrt(part_rows * lax.axis_size("gx"))
    return (state_grad, grad_pair * factor, grad_message * factor, grad_update * factor)


def solution(mesh):
    in_specs = (
        P(None, ("groups", "gx")),
        P(None, None, ("groups", "gx")),
        P(None, None, ("groups", "gx")),
        P(None, None, ("groups", "gx")),
        P(None, None, ("groups", "gx")),
        P(None, ("groups", "gx")),
        P(None, None, ("groups", "gx")),
        P(),
        P(),
        P(),
        P(),
        P(),
        P(),
        P(),
    )
    out_specs = (
        P(None, ("groups", "gx")),
        P("groups", None, None, None),
        P("groups", None, None),
        P("groups", None, None),
    )
    return jax.shard_map(local, mesh=mesh, in_specs=in_specs, out_specs=out_specs, check_vma=False)
```

profile of v0, /device:TPU:1, one launch (start us, length us, event | category | flops | bytes accessed | tf_op | source)
XLA Modules:
  0.0 866.1 jit_solution(7149604391946807298)
XLA Ops:
  11.2 4.5 collective-permute-start
  31.4 20.9 %gather_fusion.4 = f32[6144,3]{1,0:T(8,128)} fusion(f32[3,512]{0,1:T(8,128)S(1)} %copy.207, s32[6144]{0:T(1024)S(1)} %get-tuple-element.253), kind=kCustom, calls=%fused_computation.2.clone | custom fusion | bytes 172032 | tf_op jit(solution)/shard_map/jit(_take)/gather | solution.py:46
  52.3 2.4 copy.208
  56.1 20.9 %gather_fusion.3 = f32[6144,64]{1,0:T(8,128)} fusion(f32[64,512]{0,1:T(8,128)S(1)} %copy.204, s32[6144]{0:T(1024)S(1)} %get-tuple-element.253), kind=kCustom, calls=%fused_computation.1.clone | custom fusion | bytes 3170304 | tf_op jit(solution)/shard_map/jit(_take)/gather | solution.py:45
  77.1 4.7 broadcast_select_fusion.3
  83.8 3.0 bitcast_add_fusion.3
  86.8 3.4 fusion.36
  92.8 3.6 collective-permute-start.2
  96.5 2.1 collective-permute-start.3
  99.5 2.3 collective-permute-done.3
  103.0 20.9 %gather_fusion.8 = f32[6144,3]{1,0:T(8,128)} fusion(f32[3,512]{0,1:T(8,128)S(1)} %copy.217, s32[6144]{0:T(1024)S(1)} %copy-done.47), kind=kCustom, calls=%fused_computation.15.clone | custom fusion | bytes 172032 | tf_op jit(solution)/shard_map/jit(_take)/gather | solution.py:46
  124.0 2.4 copy.218
  127.8 20.9 %gather_fusion.7 = f32[6144,64]{1,0:T(8,128)} fusion(f32[64,512]{0,1:T(8,128)S(1)} %copy.214, s32[6144]{0:T(1024)S(1)} %copy-done.47), kind=kCustom, calls=%fused_computation.13.clone | custom fusion | bytes 3170304 | tf_op jit(solution)/shard_map/jit(_take)/gather | solution.py:45
  148.7 4.7 broadcast_select_fusion.2
  155.5 3.0 bitcast_add_fusion.2
  158.6 3.4 fusion.37
  166.8 2.4 collective-permute-start.5
  170.1 3.4 collective-permute-done.5
  178.8 2.6 collective-permute-start.7
  182.2 2.7 collective-permute-done.7
  186.2 20.9 %gather_fusion.14 = f32[6144,3]{1,0:T(8,128)} fusion(f32[3,512]{0,1:T(8,128)S(1)} %copy.233, s32[6144]{0:T(1024)S(1)} %copy-done.44), kind=kCustom, calls=%fused_computation.16.clone | custom fusion | bytes 172032 | tf_op jit(solution)/shard_map/jit(_take)/gather | solution.py:46
  207.1 2.4 copy.234
  211.0 20.9 %gather_fusion.13 = f32[6144,64]{1,0:T(8,128)} fusion(f32[64,512]{0,1:T(8,128)S(1)} %copy.230, s32[6144]{0:T(1024)S(1)} %copy-done.44), kind=kCustom, calls=%fused_computation.14.clone | custom fusion | bytes 3170304 | tf_op jit(solution)/shard_map/jit(_take)/gather | solution.py:45
  231.9 4.7 broadcast_select_fusion.1
  238.7 3.0 bitcast_add_fusion.1
  241.7 3.3 fusion.38
  249.8 2.4 collective-permute-start.9
  253.0 3.0 collective-permute-done.9
  257.2 21.5 %gather_fusion.18 = f32[6144,3]{1,0:T(8,128)} fusion(f32[3,512]{0,1:T(8,128)S(1)} %copy.243, s32[6144]{0:T(1024)S(1)} %copy-done.45), kind=kCustom, calls=%fused_computation.5.clone | custom fusion | bytes 172032 | tf_op jit(solution)/shard_map/jvp(jit(_take))/gather | solution.py:46
  278.7 2.4 copy.244
  281.9 20.9 %gather_fusion.17 = f32[6144,64]{1,0:T(8,128)} fusion(f32[64,512]{0,1:T(8,128)S(1)} %copy.240, s32[6144]{0:T(1024)S(1)} %copy-done.45), kind=kCustom, calls=%fused_computation.4.clone | custom fusion | bytes 3170304 | tf_op jit(solution)/shard_map/jvp(jit(_take))/gather | solution.py:45
  302.8 4.7 broadcast_select_fusion
  309.5 2.9 bitcast_add_fusion
  312.5 2.2 fusion.39
  317.3 2.9 fusion.70
  320.2 2.6 fusion.333
  323.9 2.4 copy.250
  326.3 33.5 %scatter_custom_fusion.1 = f32[64,512]{0,1:T(8,128)S(1)} fusion(s32[6144]{0:T(1024)} %get-tuple-element.258, f32[6144,64]{1,0:T(8,128)} %copy.250, f32[]{:T(128)} %constant.415.clone.1), kind=kCustom, calls=%fused_computation.225 | custom fusion | flops 393216 | bytes 131584 | tf_op jit(solution)/shard_map/transpose(jvp(jit(_take)))/scatter-add | solution.py:45
  366.2 34.0 %scatter_custom_fusion = f32[3,512]{0,1:T(8,128)} fusion(s32[6144]{0:T(1024)} %get-tuple-element.258, f32[6144,3]{1,0:T(8,128)S(1)} %copy.247, f32[]{:T(128)} %constant.415.clone.1), kind=kCustom, calls=%fused_computation.233 | custom fusion | flops 18432 | bytes 6656 | tf_op jit(solution)/shard_map/transpose(jvp(jit(_take)))/scatter-add | solution.py:46
  404.6 3.6 collective-permute-start.10
  413.4 4.4 convolution_bitcast_fusion.30
  417.8 2.6 fusion.334
  421.5 2.2 copy.265
  423.8 33.5 %scatter_custom_fusion.5 = f32[64,512]{0,1:T(8,128)S(1)} fusion(s32[6144]{0:T(1024)} %get-tuple-element.258, f32[6144,64]{1,0:T(8,128)} %copy.265, f32[]{:T(128)} %constant.415.clone.1), kind=kCustom, calls=%fused_computation.223 | custom fusion | flops 393216 | bytes 131584 | tf_op jit(solution)/shard_map/transpose(jvp(jit(_take)))/scatter-add | solution.py:45
  458.7 2.2 copy.262
  460.9 33.5 %scatter_custom_fusion.4 = f32[3,512]{0,1:T(8,128)S(1)} fusion(s32[6144]{0:T(1024)} %get-tuple-element.258, f32[6144,3]{1,0:T(8,128)} %copy.262, f32[]{:T(128)} %constant.415.clone.1), kind=kCustom, calls=%fused_computation.231 | custom fusion | flops 18432 | bytes 6656 | tf_op jit(solution)/shard_map/transpose(jvp(jit(_take)))/scatter-add | solution.py:46
  496.8 4.8 collective-permute-start.12
  510.7 3.6 collective-permute-start.14
  518.2 4.1 fusion.335
  523.5 2.2 copy.283
  525.7 33.5 %scatter_custom_fusion.12 = f32[64,512]{0,1:T(8,128)S(1)} fusion(s32[6144]{0:T(1024)} %get-tuple-element.252, f32[6144,64]{1,0:T(8,128)} %copy.283, f32[]{:T(128)} %constant.415.clone.1), kind=kCustom, calls=%fused_computation.221 | custom fusion | flops 393216 | bytes 131584 | tf_op jit(solution)/shard_map/transpose(jvp(jit(_take)))/scatter-add | solution.py:45
  564.9 34.0 %scatter_custom_fusion.11 = f32[3,512]{0,1:T(8,128)} fusion(s32[6144]{0:T(1024)} %get-tuple-element.252, f32[6144,3]{1,0:T(8,128)S(1)} %copy.280, f32[]{:T(128)} %constant.415.clone.1), kind=kCustom, calls=%fused_computation.229 | custom fusion | flops 18432 | bytes 6656 | tf_op jit(solution)/shard_map/transpose(jvp(jit(_take)))/scatter-add | solution.py:46
  602.9 4.9 fusion.56
  607.8 2.1 collective-permute-start.17
  609.8 4.2 collective-permute-start.16
  619.3 4.1 fusion.336
  624.5 2.2 copy.298
  626.7 33.5 %scatter_custom_fusion.16 = f32[64,512]{0,1:T(8,128)S(1)} fusion(s32[6144]{0:T(1024)} %get-tuple-element.252, f32[6144,64]{1,0:T(8,128)} %copy.298, f32[]{:T(128)} %constant.415.clone.1), kind=kCustom, calls=%fused_computation.219 | custom fusion | flops 393216 | bytes 131584 | tf_op jit(solution)/shard_map/transpose(jvp(jit(_take)))/scatter-add | solution.py:45
  661.7 2.2 copy.295
  663.9 33.5 %scatter_custom_fusion.15 = f32[3,512]{0,1:T(8,128)S(1)} fusion(s32[6144]{0:T(1024)} %get-tuple-element.252, f32[6144,3]{1,0:T(8,128)} %copy.295, f32[]{:T(128)} %constant.415.clone.1), kind=kCustom, calls=%fused_computation.227 | custom fusion | flops 18432 | bytes 6656 | tf_op jit(solution)/shard_map/transpose(jvp(jit(_take)))/scatter-add | solution.py:46
  698.2 3.8 fusion.53
  702.0 57.5 %psum.22 = f32[2,64,64]{2,1,0:T(8,128)S(1)} all-reduce(f32[2,64,64]{2,1,0:T(8,128)S(1)} %fusion.53), channel_id=1, replica_groups=mesh['groups'=2,'gx'=16] {'gx'}, use_global_device_ids=true, to_apply=%region_64.71 | all-reduce | flops 8192 | bytes 65536 | tf_op jit(solution)/shard_map/psum | solution.py:210
  760.1 6.9 collective-permute-start.19
  773.8 82.2 %all-reduce.19.cloned.1.call-done = (f32[2,2,64,64]{3,2,1,0:T(8,128)}, f32[2,64,128]{2,1,0:T(8,128)}) async-done(((f32[2,2,64,64]{3,2,1,0:T(8,128)}, f32[2,64,128]{2,1,0:T(8,128)}), (f32[2,2,64,64]{3,2,1,0:T(8,128)}, f32[2,64,128]{2,1,0:T(8,128)})) %all-reduce.19.cloned.1.call-update) | async-done | bytes 131088 | tf_op jit(solution)/shard_map/psum | solution.py:210
  (598 shorter events, 122.3 us)
Async XLA Ops:
  7.2 155.5 %copy-start = (f32[3,64]{1,0:T(4,128)S(1)}, f32[3,64]{1,0:T(4,128)}, u32[]{:S(2)}) copy-start(f32[3,64]{1,0:T(4,128)} %param.63) | copy-start | bytes 2308
  7.2 17.9 %copy-start.142 = (s32[1,256]{1,0:T(1,128)S(1)}, s32[1,256]{1,0:T(1,128)}, u32[]{:S(2)}) copy-start(s32[1,256]{1,0:T(1,128)} %param.55) | copy-start | bytes 3076
  7.2 18.5 %copy-start.143 = (f32[2,64]{1,0:T(2,128)S(1)}, f32[2,64]{1,0:T(2,128)}, u32[]{:S(2)}) copy-start(f32[2,64]{1,0:T(2,128)} %param.62) | copy-start | bytes 1540
  7.2 20.9 %copy-start.101 = (f32[2,6,256]{2,0,1:T(2,128)S(1)}, f32[2,6,256]{2,0,1:T(2,128)}, u32[]{:S(2)}) copy-start(f32[2,6,256]{2,0,1:T(2,128)} %param.56) | copy-start | bytes 36868
  7.2 21.5 %copy-start.85 = (s32[2,24,256]{2,1,0:T(8,128)S(1)}, s32[2,24,256]{2,1,0:T(8,128)}, u32[]{:S(2)}) copy-start(s32[2,24,256]{2,1,0:T(8,128)} %param.52) | copy-start | bytes 147460
  7.2 22.1 %copy-start.1 = (f32[2,2,64,64]{3,2,1,0:T(8,128)S(1)}, f32[2,2,64,64]{3,2,1,0:T(8,128)}, u32[]{:S(2)}) copy-start(f32[2,2,64,64]{3,2,1,0:T(8,128)} %param.58) | copy-start | bytes 196612
  7.2 848.8 %all-reduce.19.cloned.1.call-start = ((), (), s32[]{:S(2)}) async-start(), calls=%async_computation | async-start | bytes 393216 | tf_op jit(solution)/shard_map/psum | solution.py:210
  11.2 18.9 %collective-permute-start = (f32[67,128]{1,0:T(8,128)S(1)}, f32[67,128]{1,0:T(8,128)S(1)}, u32[]{:S(2)}, u32[]{:S(2)}) collective-permute-start(f32[67,128]{1,0:T(8,128)S(1)} %select_bitcast_fusion.7), channel_id=1, source_target_pairs={{0,1},{1,2},{2,3},{3,4},{4,5},{5,6},{6,7},{7,8},{8,9},{9,10},{10,1... | collective-permute-start | bytes 102920 | tf_op jit(solution)/shard_map/ppermute | solution.py:21
  16.5 13.6 %collective-permute-start.1 = (f32[67,128]{1,0:T(8,128)S(1)}, f32[67,128]{1,0:T(8,128)S(1)}, u32[]{:S(2)}, u32[]{:S(2)}) collective-permute-start(f32[67,128]{1,0:T(8,128)S(1)} %select_bitcast_fusion.6), channel_id=1, source_target_pairs={{1,0},{2,1},{3,2},{4,3},{5,4},{6,5},{7,6},{8,7},{9,8},{10,9},{11,1... | collective-permute-start | bytes 102920 | tf_op jit(solution)/shard_map/ppermute | solution.py:22
  23.9 32.3 %copy-start.46 = (s32[6144]{0:T(1024)}, s32[6144]{0:T(1024)S(1)}, u32[]{:S(2)}) copy-start(s32[6144]{0:T(1024)S(1)} %get-tuple-element.253) | copy-start | bytes 73732
  54.8 22.2 %copy-start.30 = (f32[6144,3]{0,1:T(4,128)}, f32[6144,3]{0,1:T(4,128)S(1)}, u32[]{:S(2)}) copy-start(f32[6144,3]{0,1:T(4,128)S(1)} %get-tuple-element.227) | copy-start | bytes 221188
  90.5 33.5 %copy-start.4 = (f32[256,64]{0,1:T(8,128)}, f32[256,64]{0,1:T(8,128)S(1)}, u32[]{:S(2)}) copy-start(f32[256,64]{0,1:T(8,128)S(1)} %get-tuple-element.289) | copy-start | bytes 196612
  92.8 6.6 collective-permute-start.2
  96.5 5.3 collective-permute-start.3
  162.6 23.3 %copy-start.28 = (f32[256,64]{0,1:T(8,128)}, f32[256,64]{0,1:T(8,128)S(1)}, u32[]{:S(2)}) copy-start(f32[256,64]{0,1:T(8,128)S(1)} %get-tuple-element.293) | copy-start | bytes 196612
  164.9 5.2 collective-permute-start.4
  166.8 6.6 collective-permute-start.5
  176.8 5.4 collective-permute-start.6
  178.8 6.1 collective-permute-start.7
  247.9 5.2 collective-permute-start.8
  249.8 6.2 collective-permute-start.9
  322.8 39.4 %copy-start.68 = (f32[64,256]{1,0:T(8,128)}, f32[64,256]{1,0:T(8,128)S(1)}, u32[]{:S(2)}) copy-start(f32[64,256]{1,0:T(8,128)S(1)} %get-tuple-element.305) | copy-start | bytes 196612
  323.8 36.0 %copy-start.22 = (f32[67,512]{1,0:T(8,128)S(1)}, f32[67,512]{1,0:T(8,128)}, u32[]{:S(2)}) copy-start(f32[67,512]{1,0:T(8,128)} %copy-done.21) | copy-start | bytes 411652
  323.8 39.2 %copy-start.78 = (f32[6144]{0:T(1024)S(1)}, f32[6144]{0:T(1024)}, u32[]{:S(2)}) copy-start(f32[6144]{0:T(1024)} %get-tuple-element.256) | copy-start | bytes 73732
  323.8 39.2 %copy-start.37 = (f32[6144,3]{0,1:T(4,128)S(1)}, f32[6144,3]{0,1:T(4,128)}, u32[]{:S(2)}) copy-start(f32[6144,3]{0,1:T(4,128)} %copy-done.36) | copy-start | bytes 221188
  366.2 46.3 %copy-start.7 = (f32[256,64]{0,1:T(8,128)S(1)}, f32[256,64]{0,1:T(8,128)}, u32[]{:S(2)}) copy-start(f32[256,64]{0,1:T(8,128)} %copy-done.6) | copy-start | bytes 196612
  402.7 6.4 collective-permute-start.11
  404.6 4.9 collective-permute-start.10
  421.5 35.8 %copy-start.20 = (f32[67,512]{1,0:T(8,128)S(1)}, f32[67,512]{1,0:T(8,128)}, u32[]{:S(2)}) copy-start(f32[67,512]{1,0:T(8,128)} %copy-done.19) | copy-start | bytes 411652
  421.5 36.4 %copy-start.2 = (f32[2,2,64,64]{3,2,1,0:T(8,128)S(1)}, f32[2,2,64,64]{3,2,1,0:T(8,128)}, u32[]{:S(2)}) copy-start(f32[2,2,64,64]{3,2,1,0:T(8,128)} %param.58) | copy-start | bytes 196612
  421.5 37.0 %copy-start.77 = (f32[6144]{0:T(1024)S(1)}, f32[6144]{0:T(1024)}, u32[]{:S(2)}) copy-start(f32[6144]{0:T(1024)} %get-tuple-element.254) | copy-start | bytes 73732
  421.5 37.1 %copy-start.35 = (f32[6144,3]{0,1:T(4,128)S(1)}, f32[6144,3]{0,1:T(4,128)}, u32[]{:S(2)}) copy-start(f32[6144,3]{0,1:T(4,128)} %copy-done.34) | copy-start | bytes 221188
  458.7 42.9 %copy-start.61 = (f32[64,128]{1,0:T(8,128)S(1)}, f32[64,128]{1,0:T(8,128)}, u32[]{:S(2)}) copy-start(f32[64,128]{1,0:T(8,128)} %fusion.106) | copy-start | bytes 98308
  460.9 42.0 %copy-start.91 = (f32[64,64,1]{1,0,2:T(8,128)S(1)}, f32[64,64,1]{1,0,2:T(8,128)}, u32[]{:S(2)}) copy-start(f32[64,64,1]{1,0,2:T(8,128)} %fusion.70) | copy-start | bytes 49156
  460.9 42.0 %copy-start.92 = (f32[1,64,64]{2,1,0:T(8,128)S(1)}, f32[1,64,64]{2,1,0:T(8,128)}, u32[]{:S(2)}) copy-start(f32[1,64,64]{2,1,0:T(8,128)} %convolution_bitcast_fusion.30) | copy-start | bytes 49156
  460.9 44.1 %copy-start.137 = (s32[128]{0:T(128)S(1)}, s32[128]{0:T(128)}, u32[]{:S(2)}) copy-start(s32[128]{0:T(128)} %get-tuple-element.264) | copy-start | bytes 1540
  494.9 8.7 %collective-permute-start.13 = (f32[67,128]{1,0:T(8,128)S(1)}, f32[67,128]{1,0:T(8,128)S(1)}, u32[]{:S(2)}, u32[]{:S(2)}) collective-permute-start(f32[67,128]{1,0:T(8,128)S(1)} %get-tuple-element.238), channel_id=1, source_target_pairs={{1,0},{2,1},{3,2},{4,3},{5,4},{6,5},{7,6},{8,7},{9,8},{10,9},{11,1... | collective-permute-start | bytes 102920 | tf_op jit(solution)/shard_map/ppermute | solution.py:22
  496.8 6.9 collective-permute-start.12
  508.8 7.4 collective-permute-start.15
  510.7 4.5 collective-permute-start.14
  522.4 38.5 %copy-start.69 = (f32[64,256]{1,0:T(8,128)}, f32[64,256]{1,0:T(8,128)S(1)}, u32[]{:S(2)}) copy-start(f32[64,256]{1,0:T(8,128)S(1)} %get-tuple-element.310) | copy-start | bytes 196612
  523.4 35.8 %copy-start.18 = (f32[67,512]{1,0:T(8,128)S(1)}, f32[67,512]{1,0:T(8,128)}, u32[]{:S(2)}) copy-start(f32[67,512]{1,0:T(8,128)} %copy-done.17) | copy-start | bytes 411652
  523.4 38.2 %copy-start.76 = (f32[6144]{0:T(1024)S(1)}, f32[6144]{0:T(1024)}, u32[]{:S(2)}) copy-start(f32[6144]{0:T(1024)} %get-tuple-element.250) | copy-start | bytes 73732
  523.4 38.3 %copy-start.33 = (f32[6144,3]{0,1:T(4,128)S(1)}, f32[6144,3]{0,1:T(4,128)}, u32[]{:S(2)}) copy-start(f32[6144,3]{0,1:T(4,128)} %copy-done.32) | copy-start | bytes 221188
  563.0 38.2 %copy-start.53 = (f32[64,256]{1,0:T(8,128)S(1)}, f32[64,256]{1,0:T(8,128)}, u32[]{:S(2)}) copy-start(f32[64,256]{1,0:T(8,128)} %copy-done.52) | copy-start | bytes 196612
  607.8 6.3 collective-permute-start.17
  609.8 5.3 collective-permute-start.16
  624.4 35.8 %copy-start.16 = (f32[67,512]{1,0:T(8,128)S(1)}, f32[67,512]{1,0:T(8,128)}, u32[]{:S(2)}) copy-start(f32[67,512]{1,0:T(8,128)} %copy-done.15) | copy-start | bytes 411652
  624.4 36.4 %copy-start.3 = (f32[2,2,64,64]{3,2,1,0:T(8,128)S(1)}, f32[2,2,64,64]{3,2,1,0:T(8,128)}, u32[]{:S(2)}) copy-start(f32[2,2,64,64]{3,2,1,0:T(8,128)} %param.58) | copy-start | bytes 196612
  624.4 37.0 %copy-start.75 = (f32[6144]{0:T(1024)S(1)}, f32[6144]{0:T(1024)}, u32[]{:S(2)}) copy-start(f32[6144]{0:T(1024)} %get-tuple-element.248) | copy-start | bytes 73732
  624.4 37.1 %copy-start.31 = (f32[6144,3]{0,1:T(4,128)S(1)}, f32[6144,3]{0,1:T(4,128)}, u32[]{:S(2)}) copy-start(f32[6144,3]{0,1:T(4,128)} %copy-done.30) | copy-start | bytes 221188
  661.6 36.2 %copy-start.51 = (f32[64,256]{1,0:T(8,128)S(1)}, f32[64,256]{1,0:T(8,128)}, u32[]{:S(2)}) copy-start(f32[64,256]{1,0:T(8,128)} %copy-done.50) | copy-start | bytes 196612
  661.6 36.2 %copy-start.57 = (f32[2,64,128]{2,1,0:T(8,128)S(1)}, f32[2,64,128]{2,1,0:T(8,128)}, u32[]{:S(2)}) copy-start(f32[2,64,128]{2,1,0:T(8,128)} %fusion.51) | copy-start | bytes 196612
  661.6 36.2 %copy-start.120 = (f32[256]{0:T(256)S(1)}, f32[256]{0:T(256)}, u32[]{:S(2)}) copy-start(f32[256]{0:T(256)} %copy-done.119) | copy-start | bytes 3076
  661.6 36.5 %copy-start.10 = (f32[64,24,256]{2,0,1:T(8,128)S(1)}, f32[64,24,256]{2,0,1:T(8,128)}, u32[]{:S(2)}) copy-start(f32[64,24,256]{2,0,1:T(8,128)} %copy-done.8) | copy-start | bytes 4718596
  661.6 36.5 %copy-start.65 = (f32[2,64,64]{2,1,0:T(8,128)S(1)}, f32[2,64,64]{2,1,0:T(8,128)}, u32[]{:S(2)}) copy-start(f32[2,64,64]{2,1,0:T(8,128)} %fusion.56) | copy-start | bytes 98308
  661.6 36.5 %copy-start.81 = (f32[64,256]{1,0:T(8,128)S(1)}, f32[64,256]{1,0:T(8,128)}, u32[]{:S(2)}) copy-start(f32[64,256]{1,0:T(8,128)} %copy-done.80) | copy-start | bytes 196612
  661.7 36.5 %copy-start.106 = (f32[24,256]{1,0:T(8,128)S(1)}, f32[24,256]{1,0:T(8,128)}, u32[]{:S(2)}) copy-start(f32[24,256]{1,0:T(8,128)} %get-tuple-element.245) | copy-start | bytes 73732
  698.1 73.3 %copy-start.136 = (s32[128]{0:T(128)S(1)}, s32[128]{0:T(128)}, u32[]{:S(2)}) copy-start(s32[128]{0:T(128)} %get-tuple-element.262) | copy-start | bytes 1540
  701.9 71.1 %copy-start.90 = (f32[64,3]{0,1:T(4,128)S(1)}, f32[64,3]{0,1:T(4,128)}, u32[]{:S(2)}) copy-start(f32[64,3]{0,1:T(4,128)} %param.57) | copy-start | bytes 2308
  701.9 71.1 %copy-start.117 = (f32[3,256]{1,0:T(4,128)S(1)}, f32[3,256]{1,0:T(4,128)}, u32[]{:S(2)}) copy-start(f32[3,256]{1,0:T(4,128)} %copy-done.116) | copy-start | bytes 9220
  702.0 71.3 %copy-start.112 = (f32[3,256]{1,0:T(4,128)S(1)}, f32[3,256]{1,0:T(4,128)}, u32[]{:S(2)}) copy-start(f32[3,256]{1,0:T(4,128)} %get-tuple-element.194) | copy-start | bytes 9220
  760.1 9.6 %collective-permute-start.19 = (f32[67,128]{1,0:T(8,128)S(1)}, f32[67,128]{1,0:T(8,128)S(1)}, u32[]{:S(2)}, u32[]{:S(2)}) collective-permute-start(f32[67,128]{1,0:T(8,128)S(1)} %get-tuple-element.234), channel_id=1, source_target_pairs={{1,0},{2,1},{3,2},{4,3},{5,4},{6,5},{7,6},{8,7},{9,8},{10,9},{11,1... | collective-permute-start | bytes 102920 | tf_op jit(solution)/shard_map/ppermute | solution.py:22
  767.0 3.1 collective-permute-start.18
  (111 other events, 707.8 us)
Sparse Core Ops, SparseCore 0:
  769.8 86.1 all-reduce.18
where the time goes:
time: 875 us; the launch traced here: 866 us
  other arithmetic  328 us (37%)
  local copies, waits for them, and re-layouts  229 us (26%)
  waiting for transfers between devices  95.9 us (11%)
  matrix products  79.4 us (9%)
  starting transfers between devices  58.4 us (7%)
  blocking collectives  57.5 us (7%)
  between operations  17.4 us (2%)
    scatter-add x4, other arithmetic, apply_layer(): jnp.take(joined[:3], flat_index, axis=1).reshape(3, slot_total, row_total)  135 us
    scatter-add x4, other arithmetic, apply_layer(): jnp.take(projected, flat_index, axis=1)  134 us
    gather x8, local copies, waits for them, and re-layouts, apply_layer(): jnp.take(joined[:3], flat_index, axis=1).reshape(3, slot_total, row_total)  93.8 us
    gather x4, local copies, waits for them, and re-layouts, apply_layer(): jnp.take(projected, flat_index, axis=1)  83.7 us
    psum x1, waiting for transfers between devices, local(): lax.psum((grad_pair, grad_message, grad_update), 'gx')  82.2 us
    psum x1, blocking collectives, local(): lax.psum((grad_pair, grad_message, grad_update), 'gx')  57.5 us
    dot_general x12, matrix products, apply_layer(): jnp.einsum('oh,hkp->okp', message_layer, edge_hidden, precision=HIGHEST)  41.6 us
    ppermute x10, starting transfers between devices, padded(): before = lax.ppermute(last, axis, up)  32.2 us
  transfers between devices with their start and end apart: 21, of which 9 were waited for; matrix products, arithmetic and copies ran while one was open for 3% of the time, Pallas kernels for 0%

commit v1 on v0

v1 whole, which is shorter than its diff:
```python
from functools import partial
import math

import jax
import jax.numpy as jnp
from jax import lax
from jax.experimental import pallas as pl
from jax.experimental.pallas import tpu as pltpu
from jax.sharding import PartitionSpec as P

HIGHEST = lax.Precision.HIGHEST
TIME_STEP = 0.5
EPSILON = 1e-05
F32 = jnp.float32
BF16 = jnp.bfloat16
GROUP = 4


def dot(a, b):
    return jnp.dot(a, b, precision=HIGHEST, preferred_element_type=F32)


def dot_nt(a, b, precision=HIGHEST):
    return lax.dot_general(
        a, b, (((1,), (1,)), ((), ())), precision=precision, preferred_element_type=F32
    )


def split(x):
    high = x.astype(BF16)
    low = (x - high.astype(F32)).astype(BF16)
    return high, low


def split_rows(x):
    high, low = split(x)
    return jnp.concatenate([high, low], axis=0)


def wide_weight(w):
    high = w.astype(BF16).astype(F32)
    return jnp.concatenate([high, high, w - high], axis=1).astype(BF16)


def hot(values, rows, start=0):
    count = lax.broadcasted_iota(jnp.int32, (rows, values.shape[1]), 0) + start
    return jnp.where(count == values, 1.0, 0.0).astype(BF16)


def kernel(
    size,
    chunk,
    state_ref,
    nb_ref,
    mask_ref,
    face_ref,
    mig_ref,
    order_ref,
    loss_ref,
    enc_ref,
    pair_ref,
    geo_ref,
    msg_ref,
    upd_ref,
    gain_ref,
    dec_ref,
    sg_ref,
    pg_ref,
    mg_ref,
    ug_ref,
    oh_ref,
    mrow_ref,
    q_ref,
    r_ref,
    act_ref,
    slope_ref,
    mslope_ref,
    faces_ref,
    pv_ref,
    sbuf,
    rbuf,
    gbuf,
    gather_buf,
    final_buf,
    send_sem,
    recv_sem,
    rs_send,
    rs_recv,
    ag_send,
    ag_recv,
):
    steps, slots, parts = nb_ref.shape
    layers, features = gain_ref.shape
    halo = face_ref.shape[2]
    moved = mig_ref.shape[2]
    joint = parts + 2 * halo
    wide = GROUP * parts
    groups = slots // GROUP
    block = 3 * features
    me = lax.axis_index("gx")

    def other(off):
        return lax.rem(me + off, size)

    barrier = pltpu.get_barrier_semaphore()

    def greet(off, carry):
        pl.semaphore_signal(
            barrier, inc=1, device_id={"gx": other(off)}, device_id_type=pl.DeviceIdType.MESH
        )
        return carry

    lax.fori_loop(1, size, greet, 0)

    for s in range(steps):

        def build(c, carry):
            for k in range(GROUP):
                row = c * GROUP + k
                lanes = slice(k * parts, (k + 1) * parts)
                oh_ref[s, c, :, lanes] = hot(nb_ref[s, pl.ds(row, 1), :], joint)
                mrow_ref[s, c, 0:1, lanes] = mask_ref[s, pl.ds(row, 1), :].astype(F32) * (
                    1.0 / slots
                )
            return carry

        lax.fori_loop(0, groups, build, 0)
        for d in range(2):
            faces_ref[s, :, d * halo : (d + 1) * halo] = hot(face_ref[s, d : d + 1, :], parts)

    pv_ref[...] = jnp.zeros_like(pv_ref)
    q_ref[...] = jnp.zeros_like(q_ref)
    sbuf[...] = jnp.zeros_like(sbuf)
    gbuf[...] = jnp.zeros_like(gbuf)

    @pl.when(me == 0)
    def _():
        rbuf[:, 0] = jnp.zeros(rbuf.shape[:1] + rbuf.shape[2:], F32)

    @pl.when(me == size - 1)
    def _():
        rbuf[:, 1] = jnp.zeros(rbuf.shape[:1] + rbuf.shape[2:], F32)

    pl.semaphore_wait(barrier, size - 1)

    def copies(x):
        up = pltpu.make_async_remote_copy(
            src_ref=sbuf.at[x, 0],
            dst_ref=rbuf.at[x, 0],
            send_sem=send_sem.at[x, 0],
            recv_sem=recv_sem.at[x, 0],
            device_id={"gx": me + 1},
            device_id_type=pl.DeviceIdType.MESH,
        )
        down = pltpu.make_async_remote_copy(
            src_ref=sbuf.at[x, 1],
            dst_ref=rbuf.at[x, 1],
            send_sem=send_sem.at[x, 1],
            recv_sem=recv_sem.at[x, 1],
            device_id={"gx": me - 1},
            device_id_type=pl.DeviceIdType.MESH,
        )
        return up, down

    def start(x):
        up, down = copies(x)
        pl.when(me < size - 1)(up.start)
        pl.when(me > 0)(down.start)

    def finish(x):
        up, down = copies(x)

        @pl.when(me > 0)
        def _():
            down.wait_send()
            up.wait_recv()

        @pl.when(me < size - 1)
        def _():
            up.wait_send()
            down.wait_recv()

    eye = jnp.where(
        lax.broadcasted_iota(jnp.int32, (features, features), 0)
        == lax.broadcasted_iota(jnp.int32, (features, features), 1),
        1.0,
        0.0,
    )
    encoder = enc_ref[...]
    dec_t = dot_nt(eye, dec_ref[...])
    gain_t = dot_nt(eye, gain_ref[...])

    def spread_rows(columns, rows):
        return sum(columns[:, c : c + 1] * rows[c] for c in range(3))

    def fold_rows(columns, array):
        return [
            jnp.sum(columns[:, c : c + 1] * array, axis=0, keepdims=True) for c in range(3)
        ]

    def tiled(x):
        return jnp.concatenate([x] * GROUP, axis=1)

    def slot_sum(x):
        return sum(x[:, k * parts : (k + 1) * parts] for k in range(GROUP))

    order = order_ref[0:1, :]
    order_own = hot(order, parts)
    low_code = jnp.where(order >= parts + moved, order - parts - moved + halo, order - parts)
    order_halo = hot(low_code, 2 * halo)
    going = [hot(mig_ref[0, d : d + 1, :], parts) for d in range(2)]

    def hot_dot(x, selector):
        rows = x.shape[0]
        pair = jnp.dot(split_rows(x), selector, preferred_element_type=F32)
        return pair[:rows] + pair[rows:]

    def hot_dot_nt(x, selector):
        rows = x.shape[0]
        pair = dot_nt(split_rows(x), selector, None)
        return pair[:rows] + pair[rows:]

    places = [state_ref[c : c + 1, :] for c in range(3)]
    speeds = [state_ref[c + 3 : c + 4, :] for c in range(3)]
    history = {}
    x_id = 0
    for s in range(steps):
        for c in range(3):
            pv_ref[s, c : c + 1, :] = places[c]
        own_places = pv_ref[s, 0:8]
        latent = spread_rows(encoder, speeds)
        for l in range(layers):
            geo = geo_ref[l]
            table = dot(pair_ref[l, 1], latent) + spread_rows(geo, places)
            first = l == 0
            leaving = jnp.concatenate([table, own_places], axis=0) if first else table
            sent = hot_dot(leaving, faces_ref[s])
            count = leaving.shape[0]
            sbuf[x_id, 0, :count] = sent[:, :halo]
            sbuf[x_id, 1, :count] = sent[:, halo:]
            start(x_id)
            own = dot(pair_ref[l, 0], latent) - spread_rows(geo, places)
            base_update = dot(upd_ref[l, :, :features], latent)
            weight = wide_weight(msg_ref[l])
            own_wide = tiled(own)
            places_wide = tiled(own_places)
            geo_r = geo[:, 3:4]
            finish(x_id)
            full = jnp.concatenate(
                [table, rbuf[x_id, 0, :features], rbuf[x_id, 1, :features]], axis=1
            )
            pieces = split_rows(full)
            if first:
                spots = jnp.concatenate(
                    [own_places, rbuf[x_id, 0, features:], rbuf[x_id, 1, features:]], axis=1
                )
                spots_high = spots.astype(BF16).astype(F32)
                spot_pieces = jnp.concatenate([spots_high, spots - spots_high], axis=0)
                pieces = jnp.concatenate([pieces, spot_pieces.astype(BF16)], axis=0)
            x_id += 1

            def edges(c, total):
                taken = jnp.dot(pieces, oh_ref[s, c], preferred_element_type=F32)
                senders = taken[:features] + taken[features : 2 * features]
                if first:
                    at = 2 * features
                    offsets = taken[at : at + 8] + taken[at + 8 : at + 16] - places_wide
                    squared = jnp.sum(offsets * offsets, axis=0, keepdims=True) + 1.0
                    distance = jnp.sqrt(squared)
                    r_ref[s, c, 0:1, :] = distance
                    q_ref[s, c] = offsets / distance
                else:
                    distance = r_ref[s, c, 0:1, :]
                pre = own_wide + senders + geo_r * distance
                gate = 0.5 * jnp.tanh(0.5 * pre) + 0.5
                hidden = pre * gate
                slope_ref[s, l, c] = gate + hidden - hidden * gate
                both = split_rows(hidden)
                act_ref[s, l, c] = both
                pre2 = jnp.dot(
                    weight,
                    jnp.concatenate([both, both[:features]], axis=0),
                    preferred_element_type=F32,
                )
                gate2 = 0.5 * jnp.tanh(0.5 * pre2) + 0.5
                message = pre2 * gate2
                scale = mrow_ref[s, c, 0:1, :]
                mslope_ref[s, l, c] = (gate2 + message - message * gate2) * scale
                return total + slot_sum(message * scale)

            collected = lax.fori_loop(0, groups, edges, jnp.zeros((features, parts), F32))
            update = base_update + dot(upd_ref[l, :, features:], collected)
            centred = update - jnp.mean(update, axis=0, keepdims=True)
            spread = lax.rsqrt(jnp.mean(centred * centred, axis=0, keepdims=True) + EPSILON)
            normed = centred * spread
            history[s, l] = (latent, collected, normed, spread)
            latent = latent + gain_t[:, l : l + 1] * normed
        gained = fold_rows(dec_t, latent)
        speeds = [speeds[c] + TIME_STEP * gained[c] for c in range(3)]
        places = [places[c] + TIME_STEP * speeds[c] for c in range(3)]
        if s + 1 < steps:
            for c in range(3):
                pv_ref[s, 8 + c : 9 + c, :] = places[c]
                pv_ref[s, 16 + c : 17 + c, :] = speeds[c]
            advanced = pv_ref[s, 8:24]
            for d in range(2):
                sbuf[x_id, d, :16, :moved] = hot_dot(advanced, going[d])
            start(x_id)
            kept = hot_dot(advanced, order_own)
            finish(x_id)
            arrived = jnp.concatenate([rbuf[x_id, 0, :16], rbuf[x_id, 1, :16]], axis=1)
            pv_ref[s, 8:24] = kept + hot_dot(arrived, order_halo)
            x_id += 1
            places = [pv_ref[s, 8 + c : 9 + c, :] for c in range(3)]
            speeds = [pv_ref[s, 16 + c : 17 + c, :] for c in range(3)]

    carried = [None] * 6
    for s in reversed(range(steps)):
        grad_out = [loss_ref[s, c : c + 1, :] for c in range(6)]
        if carried[0] is not None:
            grad_out = [a + b for a, b in zip(grad_out, carried)]
        grad_places = grad_out[:3]
        grad_speeds = [grad_out[3 + c] + TIME_STEP * grad_out[c] for c in range(3)]
        grad_latent = spread_rows(dec_t, [TIME_STEP * g for g in grad_speeds])
        far_total = jnp.zeros((8, joint), F32)
        near_total = jnp.zeros((8, parts), F32)
        for l in reversed(range(layers)):
            latent, collected, normed, spread = history[s, l]
            geo = geo_ref[l]
            geo_r = geo[:, 3:4]
            g_norm = gain_t[:, l : l + 1] * grad_latent
            g_update = spread * (
                g_norm
                - jnp.mean(g_norm, axis=0, keepdims=True)
                - normed * jnp.mean(g_norm * normed, axis=0, keepdims=True)
            )
            upd_collected_t = upd_ref[l, :, features:].T
            g_wide = tiled(dot(upd_collected_t, g_update))
            weight_t = wide_weight(msg_ref[l].T)

            def back(c, carry):
                spread_sum, own_sum, near_sum, weight_sum = carry
                g_pre2 = g_wide * mslope_ref[s, l, c]
                both = split_rows(g_pre2)
                weight_sum = weight_sum + dot_nt(both, act_ref[s, l, c], None)
                g_hidden = jnp.dot(
                    weight_t,
                    jnp.concatenate([both, both[:features]], axis=0),
                    preferred_element_type=F32,
                )
                g_pre = g_hidden * slope_ref[s, l, c]
                g_distance = jnp.sum(geo_r * g_pre, axis=0, keepdims=True)
                g_offset = q_ref[s, c] * g_distance
                offset_high = g_offset.astype(BF16).astype(F32)
                offset_pieces = jnp.concatenate([offset_high, g_offset - offset_high], axis=0)
                pieces = jnp.concatenate([split_rows(g_pre), offset_pieces.astype(BF16)], axis=0)
                spread_sum = spread_sum + dot_nt(pieces, oh_ref[s, c], None)
                return (
                    spread_sum,
                    own_sum + slot_sum(g_pre),
                    near_sum + slot_sum(g_offset),
                    weight_sum,
                )

            spread_sum, own_sum, near_sum, weight_sum = lax.fori_loop(
                0,
                groups,
                back,
                (
                    jnp.zeros((2 * features + 16, joint), F32),
                    jnp.zeros((features, parts), F32),
                    jnp.zeros((8, parts), F32),
                    jnp.zeros((2 * features, 2 * features), F32),
                ),
            )
            g_table = spread_sum[:features] + spread_sum[features : 2 * features]
            at = 2 * features
            far_total = far_total + spread_sum[at : at + 8] + spread_sum[at + 8 : at + 16]
            near_total = near_total + near_sum
            sbuf[x_id, 1, :features] = g_table[:, parts : parts + halo]
            sbuf[x_id, 0, :features] = g_table[:, parts + halo :]
            if l == 0:
                sbuf[x_id, 1, features:] = far_total[:, parts : parts + halo]
                sbuf[x_id, 0, features:] = far_total[:, parts + halo :]
            start(x_id)
            base = l * block
            gbuf[base + features : base + 2 * features, :] += dot_nt(
                g_update, jnp.concatenate([latent, collected], axis=0)
            )
            gbuf[base + 2 * features : base + block, :features] += (
                weight_sum[:features, :features]
                + weight_sum[features:, :features]
                + weight_sum[:features, features:]
                + weight_sum[features:, features:]
            )
            grad_latent = (
                grad_latent
                + dot(upd_ref[l, :, :features].T, g_update)
                + dot(pair_ref[l, 0].T, own_sum)
            )
            finish(x_id)
            returned = jnp.concatenate([rbuf[x_id, 1], rbuf[x_id, 0]], axis=1)
            if l > 0:
                returned = returned[:features]
            x_id += 1
            settled = hot_dot_nt(returned, faces_ref[s])
            g_table = g_table[:, :parts] + settled[:features]
            grad_latent = grad_latent + dot(pair_ref[l, 1].T, g_table)
            grad_places = [
                a + b for a, b in zip(grad_places, fold_rows(geo, g_table - own_sum))
            ]
            if l == 0:
                near = far_total[:, :parts] + settled[features:] - near_total
                grad_places = [grad_places[c] + near[c : c + 1] for c in range(3)]
            gbuf[base : base + features, :] += jnp.concatenate(
                [dot_nt(own_sum, latent), dot_nt(g_table, latent)], axis=1
            )
        grad_speeds = [
            a + b for a, b in zip(grad_speeds, fold_rows(encoder, grad_latent))
        ]
        if s > 0:
            for c in range(3):
                pv_ref[s, 8 + c : 9 + c, :] = grad_places[c]
                pv_ref[s, 16 + c : 17 + c, :] = grad_speeds[c]
            current = pv_ref[s, 8:24]
            handed = hot_dot_nt(current, order_halo)
            sbuf[x_id, 1, :16] = handed[:, :halo]
            sbuf[x_id, 0, :16] = handed[:, halo:]
            start(x_id)
            kept = hot_dot_nt(current, order_own)
            finish(x_id)
            pv_ref[s, 8:24] = (
                kept
                + hot_dot_nt(rbuf[x_id, 1, :16, :moved], going[0])
                + hot_dot_nt(rbuf[x_id, 0, :16, :moved], going[1])
            )
            x_id += 1
            carried = [pv_ref[s, 8 + c : 9 + c, :] for c in range(3)]
            carried += [pv_ref[s, 16 + c : 17 + c, :] for c in range(3)]
        else:
            for c in range(3):
                sg_ref[c : c + 1, :] = grad_places[c]
                sg_ref[3 + c : 4 + c, :] = grad_speeds[c]

    def rows_of(index):
        return pl.ds(pl.multiple_of(index * chunk, 8), chunk)

    def scatter_copy(off):
        return pltpu.make_async_remote_copy(
            src_ref=gbuf.at[rows_of(other(off))],
            dst_ref=gather_buf.at[off],
            send_sem=rs_send.at[off],
            recv_sem=rs_recv.at[off],
            device_id={"gx": other(off)},
            device_id_type=pl.DeviceIdType.MESH,
        )

    def gather_copy(off):
        return pltpu.make_async_remote_copy(
            src_ref=final_buf.at[rows_of(me)],
            dst_ref=final_buf.at[rows_of(me)],
            send_sem=ag_send.at[off],
            recv_sem=ag_recv.at[off],
            device_id={"gx": other(off)},
            device_id_type=pl.DeviceIdType.MESH,
        )

    def each(act):
        def body(off, carry):
            act(off)
            return carry

        lax.fori_loop(1, size, body, 0)

    each(lambda off: scatter_copy(off).start())

    def add(off, total):
        scatter_copy(off).wait_recv()
        return total + gather_buf[off]

    total = lax.fori_loop(1, size, add, gbuf[rows_of(me), :])
    final_buf[rows_of(me), :] = total * (1.0 / math.sqrt(parts * size))
    each(lambda off: gather_copy(off).start())

    def drain(off):
        scatter_copy(off).wait_send()
        gather_copy(off).wait_send()
        source = lax.rem(me - off + size, size)
        pltpu.make_async_remote_copy(
            src_ref=final_buf.at[rows_of(source)],
            dst_ref=final_buf.at[rows_of(source)],
            send_sem=ag_send.at[off],
            recv_sem=ag_recv.at[off],
            device_id={"gx": other(off)},
            device_id_type=pl.DeviceIdType.MESH,
        ).wait_recv()

    each(drain)
    for l in range(layers):
        base = l * block
        pg_ref[l, 0] = final_buf[base : base + features, :features]
        pg_ref[l, 1] = final_buf[base : base + features, features:]
        ug_ref[l] = final_buf[base + features : base + 2 * features, :]
        mg_ref[l] = final_buf[base + 2 * features : base + block, :features]


def local(size, *args):
    state, nb, _, face, mig = args[:5]
    pair, msg, upd = args[8], args[10], args[11]
    steps, slots, parts = nb.shape
    layers, features = msg.shape[:2]
    halo = face.shape[2]
    joint = parts + 2 * halo
    groups = slots // GROUP
    wide = GROUP * parts
    trades = 2 * steps * layers + 2 * (steps - 1)
    tiles = layers * 3 * features // 8
    chunk = -(-tiles // size) * 8
    rows = chunk * size
    vmem = pl.BlockSpec(memory_space=pltpu.VMEM)
    return pl.pallas_call(
        partial(kernel, size, chunk),
        out_shape=tuple(
            jax.ShapeDtypeStruct(a.shape, F32) for a in (state, pair, msg, upd)
        ),
        in_specs=[vmem] * len(args),
        out_specs=(vmem,) * 4,
        scratch_shapes=[
            pltpu.VMEM((steps, groups, joint, wide), BF16),
            pltpu.VMEM((steps, groups, 8, wide), F32),
            pltpu.VMEM((steps, groups, 8, wide), F32),
            pltpu.VMEM((steps, groups, 8, wide), F32),
            pltpu.VMEM((steps, layers, groups, 2 * features, wide), BF16),
            pltpu.VMEM((steps, layers, groups, features, wide), F32),
            pltpu.VMEM((steps, layers, groups, features, wide), F32),
            pltpu.VMEM((steps, parts, 2 * halo), BF16),
            pltpu.VMEM((steps, 24, parts), F32),
            pltpu.VMEM((trades, 2, features + 8, halo), F32),
            pltpu.VMEM((trades, 2, features + 8, halo), F32),
            pltpu.VMEM((rows, 128), F32),
            pltpu.VMEM((size, chunk, 128), F32),
            pltpu.VMEM((rows, 128), F32),
            pltpu.SemaphoreType.DMA((trades, 2)),
            pltpu.SemaphoreType.DMA((trades, 2)),
            pltpu.SemaphoreType.DMA((size,)),
            pltpu.SemaphoreType.DMA((size,)),
            pltpu.SemaphoreType.DMA((size,)),
            pltpu.SemaphoreType.DMA((size,)),
        ],
        compiler_params=pltpu.CompilerParams(
            collective_id=0, has_side_effects=True, vmem_limit_bytes=56 * 1024 * 1024
        ),
    )(*args)


def solution(mesh):
    block = ("groups", "gx")
    in_specs = (
        P(None, block),
        P(None, None, block),
        P(None, None, block),
        P(None, None, block),
        P(None, None, block),
        P(None, block),
        P(None, None, block),
    ) + (P(),) * 7
    out_specs = (
        P(None, block),
        P("groups", None, None, None),
        P("groups", None, None),
        P("groups", None, None),
    )
    return jax.shard_map(
        partial(local, mesh.shape["gx"]),
        mesh=mesh,
        in_specs=in_specs,
        out_specs=out_specs,
        check_vma=False,
    )
```

time: 875 us -> 94.3 us (0.11)
  other arithmetic: 328 us -> 0 us
  local copies, waits for them, and re-layouts: 229 us -> 7.17 us
  waiting for transfers between devices: 95.9 us -> 0 us
  Pallas kernels: 0 us -> 86.1 us
  matrix products: 79.4 us -> 0 us
  starting transfers between devices: 58.4 us -> 0 us
  blocking collectives: 57.5 us -> 0 us
  between operations: 17.4 us -> 0.65 us
    scatter-add x24 -> x0, other arithmetic: 285 us -> none  [the longest x4 135 us: apply_layer(): jnp.take(joined[:3], flat_index, axis=1).reshape(3, slot_total, row_total)]
    gather x34 -> x0, local copies, waits for them, and re-layouts: 187 us -> none  [the longest x8 93.8 us: apply_layer(): jnp.take(joined[:3], flat_index, axis=1).reshape(3, slot_total, row_total)]
    pallas_call x0 -> x1, Pallas kernels: none -> 86.1 us  [local(): pl.pallas_call(partial(kernel, size, chunk), out_shape=tuple((jax.ShapeDt...]
    psum x1 -> x0, waiting for transfers between devices: 82.2 us -> none  [local(): lax.psum((grad_pair, grad_message, grad_update), 'gx')]
    dot_general x63 -> x0, matrix products: 79.4 us -> none  [the longest x12 41.6 us: apply_layer(): jnp.einsum('oh,hkp->okp', message_layer, edge_hidden, precision=HIGHEST)]
    ppermute x20 -> x0, starting transfers between devices: 58.4 us -> none  [the longest x10 32.2 us: padded(): before = lax.ppermute(last, axis, up)]
    psum x1 -> x0, blocking collectives: 57.5 us -> none  [local(): lax.psum((grad_pair, grad_message, grad_update), 'gx')]
    reshape x16 -> x0, local copies, waits for them, and re-layouts: 25.8 us -> none  [the longest x12 17.8 us: apply_layer(): jnp.take(projected, flat_index, axis=1)]
  transfers between devices with their start and end apart: 21 -> 0, of which waited for: 9 -> 0; matrix products, arithmetic and copies ran while one was open for 3% -> 0% of each run, Pallas kernels for 0% -> 0%
where the time goes in v1:
time: 94.3 us; the launch traced here: 94 us
  Pallas kernels  86.1 us (91%)
  local copies, waits for them, and re-layouts  7.17 us (8%)
    pallas_call x1, Pallas kernels, local(): pl.pallas_call(partial(kernel, size, chunk), out_shape=tuple((jax.ShapeDt...  86.1 us
    unnamed x15, local copies, waits for them, and re-layouts  7.17 us

profile of v1, /device:TPU:1, one launch (start us, length us, event | category | flops | bytes accessed | tf_op | source)
XLA Modules:
  0.0 94.0 jit_solution(1583871768914211909)
XLA Ops:
  0.6 0.0 copy-start.3
  0.6 1.3 %copy.18.loss_ref = f32[2,6,256]{2,1,0:T(8,128)} copy(f32[2,6,256]{2,0,1:T(2,128)} %param.20) | data formatting | bytes 24576 | tf_op args[6]
  2.0 0.0 copy-done.3
  2.0 0.0 copy-start.2
  2.0 0.7 copy.19.enc_ref
  2.7 0.0 copy-done.2
  2.7 0.7 copy.20.geo_ref
  3.4 86.1 %shard_map.165 = (f32[6,256]{1,0:T(8,128)}, f32[2,2,64,64]{3,2,1,0:T(8,128)}, f32[2,64,64]{2,1,0:T(8,128)}, f32[2,64,128]{2,1,0:T(8,128)}) custom-call(f32[6,256]{1,0:T(8,128)} %state_ref.1, s32[2,24,256]{2,1,0:T(8,128)} %nb_ref.1, s32[2,24,256]{2,1,0:T(8,128)} %mask_ref.1, s32[2,2,128]{2,1,0:T(2,128)} %face_ref.1, s32[1,2,32]{2,1,0:T(2,128)} %mig_ref.1, ...), custom_call_target="tpu_custom_call" | custom-call | tf_op jit(solution)/shard_map/pallas_call | solution.py:521
  89.6 1.3 %copy.25 = f32[6,256]{1,0:T(8,128)} copy(f32[6,256]{1,0:T(8,128)} %get-tuple-element.8) | data formatting | bytes 12288
  90.9 0.0 copy-start.1
  90.9 1.6 %copy.26 = f32[2,2,64,64]{3,2,1,0:T(8,128)} copy(f32[2,2,64,64]{3,2,1,0:T(8,128)} %get-tuple-element.9) | data formatting | bytes 131072
  92.5 0.0 copy-done.1
  92.5 0.0 copy-start
  92.5 0.6 copy.27
  93.1 0.2 copy-done
  93.3 0.6 copy.28
Async XLA Ops:
  0.6 1.3 %copy-start.3 = (f32[64,3]{0,1:T(4,128)S(1)}, f32[64,3]{0,1:T(4,128)}, u32[]{:S(2)}) copy-start(f32[64,3]{0,1:T(4,128)} %param.21) | copy-start | bytes 2308
  2.0 0.7 copy-start.2
  90.9 1.6 %copy-start.1 = (f32[2,64,64]{2,1,0:T(8,128)S(1)}, f32[2,64,64]{2,1,0:T(8,128)}, u32[]{:S(2)}) copy-start(f32[2,64,64]{2,1,0:T(8,128)} %get-tuple-element.10) | copy-start | bytes 98308
  92.5 0.9 copy-start

commit v2 on v1

--- a/solution.py
+++ b/solution.py
@@ -13,7 +13,7 @@
 EPSILON = 1e-05
 F32 = jnp.float32
 BF16 = jnp.bfloat16
-GROUP = 4
+GROUP = 12
 
 
 def dot(a, b):
@@ -65,9 +65,7 @@
     gain_ref,
     dec_ref,
     sg_ref,
-    pg_ref,
-    mg_ref,
-    ug_ref,
+    packed_ref,
     oh_ref,
     mrow_ref,
     q_ref,
@@ -75,6 +73,8 @@
     act_ref,
     slope_ref,
     mslope_ref,
+    piece_ref,
+    message_ref,
     faces_ref,
     pv_ref,
     sbuf,
@@ -186,9 +186,14 @@
         1.0,
         0.0,
     )
-    encoder = enc_ref[...]
-    dec_t = dot_nt(eye, dec_ref[...])
-    gain_t = dot_nt(eye, gain_ref[...])
+
+    def turn(rows):
+        return dot_nt(eye, rows)
+
+    encoder = turn(enc_ref[...])
+    geometry = [turn(geo_ref[l]) for l in range(layers)]
+    dec_t = turn(dec_ref[...])
+    gain_t = turn(gain_ref[...])
 
     def spread_rows(columns, rows):
         return sum(columns[:, c : c + 1] * rows[c] for c in range(3))
@@ -230,7 +235,7 @@
         own_places = pv_ref[s, 0:8]
         latent = spread_rows(encoder, speeds)
         for l in range(layers):
-            geo = geo_ref[l]
+            geo = geometry[l]
             table = dot(pair_ref[l, 1], latent) + spread_rows(geo, places)
             first = l == 0
             leaving = jnp.concatenate([table, own_places], axis=0) if first else table
@@ -245,33 +250,50 @@
             own_wide = tiled(own)
             places_wide = tiled(own_places)
             geo_r = geo[:, 3:4]
+
+            def cut(values, spots):
+                pieces = split_rows(values)
+                if spots is None:
+                    return pieces
+                high = spots.astype(BF16).astype(F32)
+                rest = jnp.concatenate([high, spots - high], axis=0)
+                return jnp.concatenate([pieces, rest.astype(BF16)], axis=0)
+
+            def merge(taken):
+                at = 2 * features
+                values = taken[:features] + taken[features:at]
+                return values, (taken[at : at + 8] + taken[at + 8 : at + 16] if first else None)
+
+            near_pieces = cut(table, own_places if first else None)
+
+            def near_edges(c, carry):
+                senders, offsets = merge(
+                    jnp.dot(near_pieces, oh_ref[s, c, :parts], preferred_element_type=F32)
+                )
+                slope_ref[s, l, c] = own_wide + senders
+                if first:
+                    q_ref[s, c] = offsets - places_wide
+                return carry
+
+            lax.fori_loop(0, groups, near_edges, 0)
             finish(x_id)
-            full = jnp.concatenate(
-                [table, rbuf[x_id, 0, :features], rbuf[x_id, 1, :features]], axis=1
-            )
-            pieces = split_rows(full)
-            if first:
-                spots = jnp.concatenate(
-                    [own_places, rbuf[x_id, 0, features:], rbuf[x_id, 1, features:]], axis=1
+            arrived = jnp.concatenate([rbuf[x_id, 0], rbuf[x_id, 1]], axis=1)
+            far_pieces = cut(arrived[:features], arrived[features:] if first else None)
+            x_id += 1
+
+            def edges(c, total):
+                senders, offsets = merge(
+                    jnp.dot(far_pieces, oh_ref[s, c, parts:], preferred_element_type=F32)
                 )
-                spots_high = spots.astype(BF16).astype(F32)
-                spot_pieces = jnp.concatenate([spots_high, spots - spots_high], axis=0)
-                pieces = jnp.concatenate([pieces, spot_pieces.astype(BF16)], axis=0)
-            x_id += 1
-
-            def edges(c, total):
-                taken = jnp.dot(pieces, oh_ref[s, c], preferred_element_type=F32)
-                senders = taken[:features] + taken[features : 2 * features]
                 if first:
-                    at = 2 * features
-                    offsets = taken[at : at + 8] + taken[at + 8 : at + 16] - places_wide
+                    offsets = offsets + q_ref[s, c]
                     squared = jnp.sum(offsets * offsets, axis=0, keepdims=True) + 1.0
                     distance = jnp.sqrt(squared)
                     r_ref[s, c, 0:1, :] = distance
                     q_ref[s, c] = offsets / distance
                 else:
                     distance = r_ref[s, c, 0:1, :]
-                pre = own_wide + senders + geo_r * distance
+                pre = slope_ref[s, l, c] + senders + geo_r * distance
                 gate = 0.5 * jnp.tanh(0.5 * pre) + 0.5
                 hidden = pre * gate
                 slope_ref[s, l, c] = gate + hidden - hidden * gate
@@ -316,17 +338,17 @@
 
     carried = [None] * 6
     for s in reversed(range(steps)):
-        grad_out = [loss_ref[s, c : c + 1, :] for c in range(6)]
+        grad_out = [loss_ref[c, s : s + 1, :] for c in range(6)]
         if carried[0] is not None:
             grad_out = [a + b for a, b in zip(grad_out, carried)]
         grad_places = grad_out[:3]
         grad_speeds = [grad_out[3 + c] + TIME_STEP * grad_out[c] for c in range(3)]
         grad_latent = spread_rows(dec_t, [TIME_STEP * g for g in grad_speeds])
-        far_total = jnp.zeros((8, joint), F32)
+        far_total = jnp.zeros((8, 2 * halo), F32)
         near_total = jnp.zeros((8, parts), F32)
         for l in reversed(range(layers)):
             latent, collected, normed, spread = history[s, l]
-            geo = geo_ref[l]
+            geo = geometry[l]
             geo_r = geo[:, 3:4]
             g_norm = gain_t[:, l : l + 1] * grad_latent
             g_update = spread * (
@@ -339,10 +361,10 @@
             weight_t = wide_weight(msg_ref[l].T)
 
             def back(c, carry):
-                spread_sum, own_sum, near_sum, weight_sum = carry
+                spread_sum, own_sum, near_sum = carry
                 g_pre2 = g_wide * mslope_ref[s, l, c]
                 both = split_rows(g_pre2)
-                weight_sum = weight_sum + dot_nt(both, act_ref[s, l, c], None)
+                message_ref[c] = both
                 g_hidden = jnp.dot(
                     weight_t,
                     jnp.concatenate([both, both[:features]], axis=0),
@@ -354,35 +376,53 @@
                 offset_high = g_offset.astype(BF16).astype(F32)
                 offset_pieces = jnp.concatenate([offset_high, g_offset - offset_high], axis=0)
                 pieces = jnp.concatenate([split_rows(g_pre), offset_pieces.astype(BF16)], axis=0)
-                spread_sum = spread_sum + dot_nt(pieces, oh_ref[s, c], None)
+                piece_ref[c] = pieces
+                spread_sum = spread_sum + dot_nt(pieces, oh_ref[s, c, parts:], None)
                 return (
                     spread_sum,
                     own_sum + slot_sum(g_pre),
                     near_sum + slot_sum(g_offset),
-                    weight_sum,
                 )
 
-            spread_sum, own_sum, near_sum, weight_sum = lax.fori_loop(
+            spread_sum, own_sum, near_sum = lax.fori_loop(
                 0,
                 groups,
                 back,
                 (
-                    jnp.zeros((2 * features + 16, joint), F32),
+                    jnp.zeros((2 * features + 16, 2 * halo), F32),
                     jnp.zeros((features, parts), F32),
                     jnp.zeros((8, parts), F32),
+                ),
+            )
+            at = 2 * features
+            g_far = spread_sum[:features] + spread_sum[features:at]
+            far_total = far_total + spread_sum[at : at + 8] + spread_sum[at + 8 : at + 16]
+            sbuf[x_id, 1, :features] = g_far[:, :halo]
+            sbuf[x_id, 0, :features] = g_far[:, halo:]
+            if l == 0:
+                sbuf[x_id, 1, features:] = far_total[:, :halo]
+                sbuf[x_id, 0, features:] = far_total[:, halo:]
+            start(x_id)
+
+            def back_own(c, carry):
+                spread_sum, weight_sum = carry
+                return (
+                    spread_sum + dot_nt(piece_ref[c], oh_ref[s, c, :parts], None),
+                    weight_sum + dot_nt(message_ref[c], act_ref[s, l, c], None),
+                )
+
+            spread_sum, weight_sum = lax.fori_loop(
+                0,
+                groups,
+                back_own,
+                (
+                    jnp.zeros((2 * features + 16, parts), F32),
                     jnp.zeros((2 * features, 2 * features), F32),
                 ),
             )
-            g_table = spread_sum[:features] + spread_sum[features : 2 * features]
-            at = 2 * features
-            far_total = far_total + spread_sum[at : at + 8] + spread_sum[at + 8 : at + 16]
-            near_total = near_total + near_sum
-            sbuf[x_id, 1, :features] = g_table[:, parts : parts + halo]
-            sbuf[x_id, 0, :features] = g_table[:, parts + halo :]
-            if l == 0:
-                sbuf[x_id, 1, features:] = far_total[:, parts : parts + halo]
-                sbuf[x_id, 0, features:] = far_total[:, parts + halo :]
-            start(x_id)
+            g_table = spread_sum[:features] + spread_sum[features:at]
+            near_total = near_total + spread_sum[at : at + 8] + spread_sum[at + 8 : at + 16]
+            near_total = near_total - near_sum
             base = l * block
             gbuf[base + features : base + 2 * features, :] += dot_nt(
                 g_update, jnp.concatenate([latent, collected], axis=0)
@@ -404,13 +444,13 @@
                 returned = returned[:features]
             x_id += 1
             settled = hot_dot_nt(returned, faces_ref[s])
-            g_table = g_table[:, :parts] + settled[:features]
+            g_table = g_table + settled[:features]
             grad_latent = grad_latent + dot(pair_ref[l, 1].T, g_table)
             grad_places = [
                 a + b for a, b in zip(grad_places, fold_rows(geo, g_table - own_sum))
             ]
             if l == 0:
-                near = far_total[:, :parts] + settled[features:] - near_total
+                near = near_total + settled[features:]
                 grad_places = [grad_places[c] + near[c : c + 1] for c in range(3)]
             gbuf[base : base + features, :] += jnp.concatenate(
                 [dot_nt(own_sum, latent), dot_nt(g_table, latent)], axis=1
@@ -496,12 +536,18 @@
         ).wait_recv()
 
     each(drain)
+    packed_ref[...] = final_buf[...]
+
+
+def unpack(state_ref, packed_ref, sg_ref, pg_ref, mg_ref, ug_ref):
+    layers, features = mg_ref.shape[:2]
+    sg_ref[...] = state_ref[...]
     for l in range(layers):
-        base = l * block
-        pg_ref[l, 0] = final_buf[base : base + features, :features]
-        pg_ref[l, 1] = final_buf[base : base + features, features:]
-        ug_ref[l] = final_buf[base + features : base + 2 * features, :]
-        mg_ref[l] = final_buf[base + 2 * features : base + block, :features]
+        base = l * 3 * features
+        pg_ref[l, 0] = packed_ref[base : base + features, :features]
+        pg_ref[l, 1] = packed_ref[base : base + features, features:]
+        ug_ref[l] = packed_ref[base + features : base + 2 * features, :]
+        mg_ref[l] = packed_ref[base + 2 * features : base + 3 * features, :features]
 
 
 def local(size, *args):
@@ -518,13 +564,18 @@
     chunk = -(-tiles // size) * 8
     rows = chunk * size
     vmem = pl.BlockSpec(memory_space=pltpu.VMEM)
-    return pl.pallas_call(
+    args = list(args)
+    args[6] = jnp.transpose(args[6], (1, 0, 2))
+    args[7] = args[7].T
+    args[9] = jnp.transpose(args[9], (0, 2, 1))
+    grads = pl.pallas_call(
         partial(kernel, size, chunk),
-        out_shape=tuple(
-            jax.ShapeDtypeStruct(a.shape, F32) for a in (state, pair, msg, upd)
+        out_shape=(
+            jax.ShapeDtypeStruct(state.shape, F32),
+            jax.ShapeDtypeStruct((rows, 128), F32),
         ),
         in_specs=[vmem] * len(args),
-        out_specs=(vmem,) * 4,
+        out_specs=(vmem,) * 2,
         scratch_shapes=[
             pltpu.VMEM((steps, groups, joint, wide), BF16),
             pltpu.VMEM((steps, groups, 8, wide), F32),
@@ -533,6 +584,8 @@
             pltpu.VMEM((steps, layers, groups, 2 * features, wide), BF16),
             pltpu.VMEM((steps, layers, groups, features, wide), F32),
             pltpu.VMEM((steps, layers, groups, features, wide), F32),
+            pltpu.VMEM((groups, 2 * features + 16, wide), BF16),
+            pltpu.VMEM((groups, 2 * features, wide), BF16),
             pltpu.VMEM((steps, parts, 2 * halo), BF16),
             pltpu.VMEM((steps, 24, parts), F32),
             pltpu.VMEM((trades, 2, features + 8, halo), F32),
@@ -551,6 +604,14 @@
             collective_id=0, has_side_effects=True, vmem_limit_bytes=56 * 1024 * 1024
         ),
     )(*args)
+    return pl.pallas_call(
+        unpack,
+        out_shape=tuple(
+            jax.ShapeDtypeStruct(a.shape, F32) for a in (state, pair, msg, upd)
+        ),
+        in_specs=[vmem] * 2,
+        out_specs=(vmem,) * 4,
+    )(*grads)
 
 
 def solution(mesh):

time: 94.3 us -> 73.3 us (0.78)
  Pallas kernels: 86.1 us -> 72.4 us
  local copies, waits for them, and re-layouts: 7.17 us -> 0 us
    pallas_call x1 -> x2, Pallas kernels: 86.1 us -> 72.4 us  [the longest x1 70.7 us: local(): pl.pallas_call(partial(kernel, size, chunk), out_shape=(jax.ShapeDtypeStr...]
    unnamed x15 -> x0, local copies, waits for them, and re-layouts: 7.17 us -> none
where the time goes in v2:
time: 73.3 us; the launch traced here: 73.1 us
  Pallas kernels  72.4 us (99%)
    pallas_call x1, Pallas kernels, local(): pl.pallas_call(partial(kernel, size, chunk), out_shape=(jax.ShapeDtypeStr...  70.7 us
    pallas_call x1, Pallas kernels, local(): pl.pallas_call(unpack, out_shape=tuple((jax.ShapeDtypeStruct(a.shape, F32...  1.7 us

profile of v2, /device:TPU:1, one launch (start us, length us, event | category | flops | bytes accessed | tf_op | source)
XLA Modules:
  0.0 73.1 jit_solution(16233493149958622286)
XLA Ops:
  0.6 70.7 %shard_map.165 = (f32[6,256]{1,0:T(8,128)}, f32[384,128]{1,0:T(8,128)}) custom-call(f32[6,256]{1,0:T(8,128)} %state_ref.1, s32[2,24,256]{2,1,0:T(8,128)} %nb_ref.1, s32[2,24,256]{2,1,0:T(8,128)} %mask_ref.1, s32[2,2,128]{2,1,0:T(2,128)} %face_ref.1, s32[1,2,32]{2,1,0:T(2,128)} %mig_ref.1, s32[1,256]{1,0:T(1,128)} %order_ref.1, f32[6,2,256]{2,1,0:T(2,128)} %bitcast.3, ...), custom_call_target="tpu_custom_call" | custom-call | tf_op jit(solution)/shard_map/pallas_call | solution.py:571
  71.4 1.7 %shard_map.166 = (f32[6,256]{1,0:T(8,128)}, f32[2,2,64,64]{3,2,1,0:T(8,128)}, f32[2,64,64]{2,1,0:T(8,128)}, f32[2,64,128]{2,1,0:T(8,128)}) custom-call(f32[6,256]{1,0:T(8,128)} %get-tuple-element.6.state_ref, f32[384,128]{1,0:T(8,128)} %get-tuple-element.7.packed_ref), custom_call_target="tpu_custom_call" | custom-call | tf_op jit(solution)/shard_map/pallas_call | solution.py:607

commit v3 on v2

--- a/solution.py
+++ b/solution.py
@@ -16,10 +16,6 @@
 GROUP = 12
 
 
-def dot(a, b):
-    return jnp.dot(a, b, precision=HIGHEST, preferred_element_type=F32)
-
-
 def dot_nt(a, b, precision=HIGHEST):
     return lax.dot_general(
         a, b, (((1,), (1,)), ((), ())), precision=precision, preferred_element_type=F32
@@ -40,6 +36,12 @@
 def wide_weight(w):
     high = w.astype(BF16).astype(F32)
     return jnp.concatenate([high, high, w - high], axis=1).astype(BF16)
+
+
+def dot(a, b):
+    high, low = split(b)
+    pieces = jnp.concatenate([high, low, high], axis=0)
+    return jnp.dot(wide_weight(a), pieces, preferred_element_type=F32)
 
 
 def hot(values, rows, start=0):

time: 73.3 us -> 72 us (0.982)
  Pallas kernels: 72.4 us -> 71.1 us
    pallas_call x1, Pallas kernels: 70.7 us -> 69.4 us  [local(): pl.pallas_call(partial(kernel, size, chunk), out_shape=(jax.ShapeDtypeStr...]
where the time goes in v3:
time: 72 us; the launch traced here: 71.8 us
  Pallas kernels  71.1 us (99%)
    pallas_call x1, Pallas kernels, local(): pl.pallas_call(partial(kernel, size, chunk), out_shape=(jax.ShapeDtypeStr...  69.4 us
    pallas_call x1, Pallas kernels, local(): pl.pallas_call(unpack, out_shape=tuple((jax.ShapeDtypeStruct(a.shape, F32...  1.7 us

profile of v3, /device:TPU:1, one launch (start us, length us, event | category | flops | bytes accessed | tf_op | source)
XLA Modules:
  0.0 71.8 jit_solution(6098718964014782153)
XLA Ops:
  0.6 69.4 %shard_map.165 = (f32[6,256]{1,0:T(8,128)}, f32[384,128]{1,0:T(8,128)}) custom-call(f32[6,256]{1,0:T(8,128)} %state_ref.1, s32[2,24,256]{2,1,0:T(8,128)} %nb_ref.1, s32[2,24,256]{2,1,0:T(8,128)} %mask_ref.1, s32[2,2,128]{2,1,0:T(2,128)} %face_ref.1, s32[1,2,32]{2,1,0:T(2,128)} %mig_ref.1, s32[1,256]{1,0:T(1,128)} %order_ref.1, f32[6,2,256]{2,1,0:T(2,128)} %bitcast.3, ...), custom_call_target="tpu_custom_call" | custom-call | tf_op jit(solution)/shard_map/pallas_call | solution.py:573
  70.1 1.7 %shard_map.166 = (f32[6,256]{1,0:T(8,128)}, f32[2,2,64,64]{3,2,1,0:T(8,128)}, f32[2,64,64]{2,1,0:T(8,128)}, f32[2,64,128]{2,1,0:T(8,128)}) custom-call(f32[6,256]{1,0:T(8,128)} %get-tuple-element.6.state_ref, f32[384,128]{1,0:T(8,128)} %get-tuple-element.7.packed_ref), custom_call_target="tpu_custom_call" | custom-call | tf_op jit(solution)/shard_map/pallas_call | solution.py:609
